TPU v7x, 32 devices: a whole 2x2x4 slice. The times are simulated.
32 devices in a mesh: ctx: 8 (over z, y), head: 4 (over x, core).
Axes of the slice: x: 2, y: 2, z: 4, core: 2. Of those that a mesh axis runs over, the one named last changes fastest.
Arguments:
- queries: bfloat16 [1024, 4096], P('ctx', 'head'), may hold values from -30 to 30
- key_proj: bfloat16 [1024, 1024], P('ctx', 'head'), may hold values from -6 to 6
- value_proj: bfloat16 [1024, 1024], P('ctx', 'head'), may hold values from -6 to 6
- lengths: int32 [8], replicated, may hold values from 1 to 512, 1024 in all
- out_weight: bfloat16 [4096, 8192], P(None, 'head'), may hold values from -0.09375 to 0.09375
Outputs:
- mixed_out: bfloat16 [1024, 8192], P('ctx', 'head')
Inputs may be any that keep to these rules, and one draw needn't show every extreme that they name: Document lengths in pack order; they sum to 1024 and the longest is exactly 512.
All inputs are finite; a program needn't handle non-finite values.
Results may differ from a plain program's by a relative error of at most 0.005.
The roundings to bfloat16 on the way count: a program that leaves them out, or rounds other values in their place, can miss the bound.
Values may be sent and summed in bfloat16 or wider, within the bound.
A program may use at most 64 MiB of HBM per device.

v0:
```python
import jax
import jax.numpy as jnp
from jax import lax
from jax.sharding import PartitionSpec as P

HD = 128


rope_theta = 500000.0


def doc_starts(lengths, positions):
    doc_ends = jnp.cumsum(lengths)
    picked = jnp.where(doc_ends[None, :] <= positions[:, None], lengths[None, :], 0)
    return jnp.sum(picked, axis=1)


def rotary(projected, offsets, head_dim):
    token_count = projected.shape[0]
    heads_grid = projected.astype(jnp.float32).reshape(token_count, -1, head_dim)
    half_dim = head_dim // 2
    inverse = rope_theta ** (-2.0 * jnp.arange(half_dim).astype(jnp.float32) / head_dim)
    angles = offsets.astype(jnp.float32)[:, None] * inverse[None, :]
    cosine = jnp.cos(angles)[:, None, :]
    sine_part = jnp.sin(angles)[:, None, :]
    first_half = heads_grid[..., :half_dim]
    second_half = heads_grid[..., half_dim:]
    rotated = jnp.concatenate(
        [
            first_half * cosine - second_half * sine_part,
            second_half * cosine + first_half * sine_part,
        ],
        axis=-1,
    )
    return rotated.reshape(token_count, -1).astype(jnp.bfloat16)


def on_device(queries, key_proj, value_proj, lengths, out_weight):
    tok_rows = queries.shape[0]
    kv_local = key_proj.shape[1] // HD
    query_group = queries.shape[1] // key_proj.shape[1]
    first_row = lax.axis_index("ctx") * tok_rows
    positions = first_row + jnp.arange(tok_rows, dtype=jnp.int32)
    starts = doc_starts(lengths, positions)
    offsets = positions - starts
    q_rot = rotary(queries, offsets, HD).reshape(tok_rows, kv_local, query_group, HD)
    k_rot = rotary(key_proj, offsets, HD)
    lowest = starts[0]
    initial = (
        jnp.full((kv_local, query_group, tok_rows), -1e30, jnp.float32),
        jnp.zeros((kv_local, query_group, tok_rows), jnp.float32),
        jnp.zeros((kv_local, query_group, tok_rows, HD), jnp.float32),
    )
    begin_row = jnp.int32(0)
    key_part = lax.all_gather(k_rot, "ctx", axis=0, tiled=True)
    value_part = lax.all_gather(value_proj, "ctx", axis=0, tiled=True)
    key_count = key_part.shape[0]

    def update(state):
        running_max, running_sum, weighted = state
        key_block = key_part.reshape(key_count, kv_local, HD)
        value_block = value_part.reshape(key_count, kv_local, HD)
        scores = jnp.einsum(
            "tkgd,nkd->kgtn", q_rot, key_block, preferred_element_type=jnp.float32
        ) / jnp.sqrt(jnp.float32(HD))
        key_pos = jnp.arange(key_count, dtype=jnp.int32)
        allowed = (key_pos[None, :] <= positions[:, None]) & (key_pos[None, :] >= starts[:, None])
        scores = jnp.where(allowed, scores, -1e30)
        new_max = jnp.maximum(running_max, jnp.max(scores, axis=-1))
        weights = jnp.where(allowed, jnp.exp(scores - new_max[..., None]), 0.0)
        new_sum = jnp.sum(weights, axis=-1)
        product = jnp.einsum(
            "kgtn,nkd->kgtd",
            weights.astype(jnp.bfloat16),
            value_block,
            preferred_element_type=jnp.float32,
        )
        return (new_max, new_sum, product)

    needed = (begin_row <= first_row + tok_rows - 1) & (begin_row + key_count - 1 >= lowest)
    state = lax.cond(needed, update, lambda state: state, initial)
    running_max, running_sum, weighted = state
    normed = (weighted / running_sum[..., None]).astype(jnp.bfloat16)
    attended = jnp.transpose(normed, (2, 0, 1, 3)).reshape(tok_rows, kv_local * query_group * HD)
    mixed_out = jnp.dot(
        lax.all_gather(attended, "head", axis=1, tiled=True),
        out_weight,
        preferred_element_type=jnp.float32,
    )
    return mixed_out.astype(jnp.bfloat16)


def solution(mesh):
    placed = (P("ctx", "head"), P("ctx", "head"), P("ctx", "head"), P(), P(None, "head"))
    return jax.shard_map(
        on_device, mesh=mesh, in_specs=placed, out_specs=P("ctx", "head"), check_vma=False
    )
```

profile of v0, /device:TPU:25, one launch (start us, length us, event | category | flops | bytes accessed | tf_op | source)
XLA Modules:
  0.0 117.2 jit_solution(12534051568828485983)
XLA Ops:
  6.5 0.0 all-gather.2.cloned.1.call-start
  6.5 0.8 reduce-window.8
  7.4 0.7 select_reduce_fusion
  8.1 1.1 copy.22
  9.3 0.2 multiply_cosine_fusion
  9.5 0.1 copy.20
  9.6 0.1 copy.21
  9.7 0.1 multiply_subtract_fusion
  9.8 0.9 reshape.132
  10.7 0.3 subtract_convert_fusion
  11.0 0.2 pad_maximum_fusion.1
  11.2 23.1 %all_gather.9 = bf16[1024,256]{1,0:T(8,128)(2,1)S(1)} all-gather(bf16[128,256]{1,0:T(8,128)(2,1)S(1)} %bitcast.36), channel_id=1, replica_groups=mesh['ctx'=8,'head'=4] {'ctx'}, dimensions={0}, use_global_device_ids=true | all-gather | bytes 589824 | tf_op jit(solution)/shard_map/all_gather | solution.py:55
  34.3 26.0 %all_gather.10 = bf16[1024,256]{1,0:T(8,128)(2,1)S(1)} all-gather(bf16[128,256]{1,0:T(8,128)(2,1)} %param.9), channel_id=1, replica_groups=mesh['ctx'=8,'head'=4] {'ctx'}, dimensions={0}, use_global_device_ids=true | all-gather | bytes 589824 | tf_op jit(solution)/shard_map/all_gather | solution.py:56
  60.3 7.8 %conditional.1 = (f32[2,4,128]{2,1,0:T(4,128)S(1)}, f32[2,4,128,128]{2,3,1,0:T(8,128)S(1)}) conditional(s32[]{:T(128)} %convert_element_type.42, () %tuple.13, (s32[]{:T(128)}, s32[128]{0:T(128)S(1)}, s32[128]{0:T(128)S(1)}, bf16[1024,256]{1,0:T(8,128)(2,1)S(1)}, bf16[128,8,128]{0,2,1:T(8,128)(2,1)S(1)}, ...), branch_computations={%region_2.3_spmd, %region_3.6_spmd} | conditional | flops 550894720 | bytes 34367536 | solution.py:81
  60.3 0.1 fusion.9
  60.5 0.1 reshape.115
  60.6 0.2 copy.23
  60.8 2.7 %fusion = (f32[2,4,128]{2,1,0:T(4,128)S(1)}, f32[2,1024,128,4]{2,1,3,0:T(8,128)}) fusion(pred[128,1024]{0,1:T(8,128)(4,1)S(1)} %fusion.9, bf16[128,2,4,128]{3,0,2,1:T(8,128)(2,1)S(1)} %bitcast.32, bf16[1024,2,128,1]{2,1,0,3:T(2,128)(2,1)S(1)} %bitcast.30), kind=kOutput, calls=%fused_computation.2 | convolution fusion | flops 271580160 | bytes 5115904 | tf_op jit(solution)/shard_map/cond/branch_1_fun/tkgd,nkd->kgtn/dot_general | solution.py:63
  63.5 0.1 reshape.116
  63.6 0.0 copy-start
  63.6 3.4 %fusion.3 = f32[2,4,128,128]{2,3,1,0:T(8,128)S(1)} fusion(f32[2,1024,128,4]{2,1,3,0:T(8,128)} %get-tuple-element.45, f32[2,4,128]{2,1,0:T(4,128)S(1)} %broadcast_maximum_fusion, pred[128,1024]{0,1:T(8,128)(4,1)S(1)} %fusion.9, bf16[1024,2,128,1]{2,1,0,3:T(2,128)(2,1)S(1)} %bitcast.34), kind=kOutput, calls=%fused_computation.5 | convolution fusion | flops 273678336 | bytes 5378048 | tf_op jit(solution)/shard_map/cond | solution.py:81
  67.0 0.0 copy-done
  67.1 1.0 fusion.2
  68.1 0.8 divide_convert_fusion
  68.8 0.0 all-gather.2.cloned.1.call-update
  68.9 32.2 %all-gather.2.cloned.1.call-done = bf16[128,4096]{0,1:T(8,128)(2,1)} async-done(((bf16[128,1024]{0,1:T(8,128)(2,1)}), bf16[128,4096]{0,1:T(8,128)(2,1)}) %all-gather.2.cloned.1.call-update) | async-done | bytes 1048592 | tf_op jit(solution)/shard_map/all_gather | solution.py:86
  101.1 9.3 %convolution_convert_fusion = bf16[128,2048]{1,0:T(8,128)(2,1)} fusion(bf16[128,4096]{0,1:T(8,128)(2,1)} %all-gather.2.cloned.1.call-done, bf16[4096,2048]{1,0:T(8,128)(2,1)} %param.11), kind=kOutput, calls=%fused_computation.18 | convolution fusion | flops 2147745792 | bytes 18350080 | tf_op jit(solution)/shard_map/dot_general | solution.py:85
  (9 shorter events, 0.1 us)
Async XLA Ops:
  6.5 94.6 %all-gather.2.cloned.1.call-start = ((), (), s32[]{:S(2)}) async-start(), calls=%async_computation | async-start | bytes 1310720 | tf_op jit(solution)/shard_map/all_gather | solution.py:86
  63.6 3.5 %copy-start = (f32[2,1024,128,4]{2,1,3,0:T(8,128)S(1)}, f32[2,1024,128,4]{2,1,3,0:T(8,128)}, u32[]{:S(2)}) copy-start(f32[2,1024,128,4]{2,1,3,0:T(8,128)} %get-tuple-element.45) | copy-start | bytes 12582916 | tf_op jit(solution)/shard_map/cond
Sparse Core Ops, SparseCore 0:
  69.0 32.0 all-gather.1
where the time goes:
time: 119 us; the launch traced here: 117 us
  blocking collectives  49 us (41%)
  waiting for transfers between devices  32.2 us (27%)
  matrix products  15.4 us (13%)
  between operations  13.5 us (11%)
  other arithmetic  4.3 us (4%)
  local copies, waits for them, and re-layouts  2.66 us (2%)
    all_gather x1, waiting for transfers between devices, on_device(): lax.all_gather(attended, 'head', axis=1, tiled=True)  32.2 us
    all_gather x1, blocking collectives, on_device(): value_part = lax.all_gather(value_proj, 'ctx', axis=0, tiled=True)  26 us
    all_gather x1, blocking collectives, on_device(): key_part = lax.all_gather(k_rot, 'ctx', axis=0, tiled=True)  23.1 us
    dot_general x1, matrix products, on_device(): jnp.dot(lax.all_gather(attended, 'head', axis=1, tiled=True), out_weight,...  9.26 us
    cond x1, matrix products, on_device(): state = lax.cond(needed, update, lambda state: state, initial)  3.43 us
    dot_general x1, matrix products, update(): jnp.einsum('tkgd,nkd->kgtn', q_rot, key_block, preferred_element_type=jnp...  2.68 us
  transfers between devices with their start and end apart: 1, of which 1 were waited for; matrix products, arithmetic and copies ran while one was open for 0% of the time, Pallas kernels for 0%

commit v1 on v0

v1 whole, which is shorter than its diff:
```python
import functools

import jax
import jax.numpy as jnp
from jax import lax
from jax.experimental import pallas as pl
from jax.experimental.pallas import tpu as pltpu
from jax.sharding import PartitionSpec as P

HD = 128
ROPE_THETA = 500000.0
MESH = pl.DeviceIdType.MESH


def kernel(
    n, heads, window, lengths, inverse, q_in, k_in, v_in, w_hbm, out,
    kv, q_rot, att, w, acc,
    w_sem, z_send, y_send, kv_recv, x_send, s_send, r_send, att_recv,
):
    tok = q_in.shape[0]
    groups = k_in.shape[1] // HD
    per = q_in.shape[1] // k_in.shape[1]
    wide = per * HD
    steps = window // 2
    chips = heads // 2
    ctx, head = lax.axis_index("ctx"), lax.axis_index("head")
    col, core = lax.rem(ctx, 2), lax.rem(head, 2)
    chip = head // 2
    partner = ctx + 1 - 2 * col
    sibling = head + 1 - 2 * core

    barrier = pltpu.get_barrier_semaphore()

    def greet(c, h):
        pl.semaphore_signal(barrier, inc=1, device_id=(c, h), device_id_type=MESH)

    expected = jnp.int32(2 + chips - 1)
    greet(partner, head)
    greet(ctx, sibling)
    for s in range(1, chips):
        greet(ctx, lax.rem(chip + s, chips) * 2 + core)
    for k in range(1, steps + 1):
        up, down = ctx + 2 * k < n, ctx - 2 * k >= 0
        expected = expected + up.astype(jnp.int32) + down.astype(jnp.int32)

        @pl.when(up)
        def _():
            greet(ctx + 2 * k, head)

        @pl.when(down)
        def _():
            greet(ctx - 2 * k, head)

    def weight_copy(h, g):
        piece = h * groups + g
        rows = pl.ds(pl.multiple_of(piece * wide, wide), wide)
        return pltpu.make_async_copy(w_hbm.at[rows, :], w.at[piece], w_sem.at[piece])

    order = []
    for s in range(chips):
        order.append(lax.rem(chip + s, chips) * 2 + core)
    for s in range(chips):
        order.append(lax.rem(chip + s, chips) * 2 + 1 - core)
    for h in order:
        for g in range(groups):
            weight_copy(h, g).start()

    pos = ctx * tok + lax.broadcasted_iota(jnp.int32, (tok, HD), 0)
    starts = jnp.zeros((tok, HD), jnp.int32)
    end = jnp.int32(0)
    for j in range(lengths.shape[0]):
        end = end + lengths[j]
        starts = jnp.where(pos >= end, end, starts)
    angle = (pos - starts).astype(jnp.float32) * inverse[...]
    cosine = jnp.cos(angle)
    sine = jnp.sin(angle)
    lane = lax.broadcasted_iota(jnp.int32, (tok, HD), 1)
    sine = jnp.where(lane < HD // 2, -sine, sine)

    def rotate(x):
        x = x.astype(jnp.float32)
        return (x * cosine + pltpu.roll(x, HD // 2, 1) * sine).astype(jnp.bfloat16)

    for g in range(groups):
        cols = pl.ds(g * HD, HD)
        kv[g, 0, pl.ds(0, tok), :] = rotate(k_in[:, cols])
        kv[g, 1, pl.ds(0, tok), :] = v_in[:, cols]

    def slot(g, d):
        return kv.at[g, :, pl.ds(pl.multiple_of(d * tok, tok), tok), :]

    def z_copy(k, g):
        return pltpu.make_async_remote_copy(
            src_ref=slot(g, 0), dst_ref=slot(g, 2 * k),
            send_sem=z_send.at[k - 1, g], recv_sem=kv_recv.at[2 * k, g],
            device_id=(ctx + 2 * k, head), device_id_type=MESH,
        )

    def y_copy(m, g):
        return pltpu.make_async_remote_copy(
            src_ref=slot(g, 2 * m + 2 * col), dst_ref=slot(g, 2 * m + 1),
            send_sem=y_send.at[m, g], recv_sem=kv_recv.at[2 * m + 1, g],
            device_id=(partner, head), device_id_type=MESH,
        )

    pl.semaphore_wait(barrier, expected)

    for g in range(groups):
        for k in range(1, steps + 1):

            @pl.when(ctx + 2 * k < n)
            def _():
                z_copy(k, g).start()

        @pl.when(col == 0)
        def _():
            y_copy(0, g).start()

    for d in range(1, window + 1):

        @pl.when(ctx < d)
        def _():
            for g in range(groups):
                kv[g, :, pl.ds(d * tok, tok), :] = jnp.zeros((2, tok, HD), jnp.bfloat16)

    for j in range(groups * per):
        g, r = divmod(j, per)
        q_rot[g, pl.ds(r * tok, tok), :] = rotate(q_in[:, pl.ds(j * HD, HD)])

    def relay(g):
        for k in range(1, steps + 1):

            @pl.when(ctx - 2 * k >= 0)
            def _():
                z_copy(k, g).wait_recv()

            if k <= steps - 1:

                @pl.when((col == 0) & (ctx - 2 * k >= 0))
                def _():
                    y_copy(k, g).start()

            @pl.when((col == 1) & (ctx - 2 * k >= 0))
            def _():
                y_copy(k - 1, g).start()

    keys = (window + 1) * tok
    spot = lax.broadcasted_iota(jnp.int32, (tok, keys), 1)
    back = spot // tok
    key_pos = (ctx - back) * tok + (spot - back * tok)
    allowed = (key_pos <= pos[:, :1]) & (key_pos >= starts[:, :1])
    scale = jnp.float32(HD ** -0.5)

    def attend(g):
        for m in range(steps):

            @pl.when(ctx - 2 * m - 1 >= 0)
            def _():
                y_copy(m, g).wait_recv()

        scores = lax.dot_general(
            q_rot[g], kv[g, 0], (((1,), (1,)), ((), ())), preferred_element_type=jnp.float32
        )
        for r in range(per):
            one = jnp.where(allowed, scores[r * tok:(r + 1) * tok] * scale, -1e30)
            expo = jnp.exp(one - jnp.max(one, axis=-1, keepdims=True))
            total = jnp.sum(expo, axis=-1, keepdims=True)
            mixed = jnp.dot(
                expo.astype(jnp.bfloat16), kv[g, 1], preferred_element_type=jnp.float32
            )
            att[head, g, :, pl.ds(r * HD, HD)] = (mixed / total).astype(jnp.bfloat16)

    def x_copy(s, g):
        return pltpu.make_async_remote_copy(
            src_ref=att.at[head, g], dst_ref=att.at[head, g],
            send_sem=x_send.at[s - 1, g], recv_sem=att_recv.at[head, g],
            device_id=(ctx, lax.rem(chip + s, chips) * 2 + core), device_id_type=MESH,
        )

    def core_copy(h, g, sem):
        return pltpu.make_async_remote_copy(
            src_ref=att.at[h, g], dst_ref=att.at[h, g],
            send_sem=sem, recv_sem=att_recv.at[h, g],
            device_id=(ctx, sibling), device_id_type=MESH,
        )

    def arrived(h, g):
        core_copy(h, g, s_send.at[g]).wait_recv()

    def share(g):
        for s in range(1, chips):
            x_copy(s, g).start()
        core_copy(head, g, s_send.at[g]).start()

    def project(h, g, first=False):
        weight_copy(h, g).wait()
        part = jnp.dot(att[h, g], w[h * groups + g], preferred_element_type=jnp.float32)
        acc[...] = part if first else acc[...] + part

    relay(0)
    for g in range(groups):
        if g + 1 < groups:
            relay(g + 1)
        attend(g)
        share(g)
    for g in range(groups):
        project(head, g, first=g == 0)
    for g in range(groups):
        arrived(sibling, g)
        project(sibling, g)
    for g in range(groups):
        for s in range(1, chips):
            h = order[s]
            arrived(h, g)
            core_copy(h, g, r_send.at[s - 1, g]).start()
            project(h, g)
        for s in range(1, chips):
            h = order[chips + s]
            arrived(h, g)
            project(h, g)
    out[...] = acc[...].astype(out.dtype)

    for g in range(groups):
        for k in range(1, steps + 1):

            @pl.when(ctx + 2 * k < n)
            def _():
                z_copy(k, g).wait_send()

        for m in range(steps):

            @pl.when(ctx - 2 * m - 2 * col >= 0)
            def _():
                y_copy(m, g).wait_send()

        for s in range(1, chips):
            x_copy(s, g).wait_send()
            core_copy(order[s], g, r_send.at[s - 1, g]).wait_send()
        core_copy(head, g, s_send.at[g]).wait_send()


def on_device(n, heads, queries, key_proj, value_proj, lengths, out_weight):
    tok = queries.shape[0]
    groups = key_proj.shape[1] // HD
    wide = queries.shape[1] // groups
    columns = out_weight.shape[1]
    window = n // 2
    half = -2.0 * jnp.arange(HD // 2).astype(jnp.float32) / HD
    inverse = ROPE_THETA ** half
    inverse = jnp.concatenate([inverse, inverse])[None, :]
    vmem = pl.BlockSpec(memory_space=pltpu.VMEM)
    dma = pltpu.SemaphoreType.DMA
    return pl.pallas_call(
        functools.partial(kernel, n, heads, window),
        out_shape=jax.ShapeDtypeStruct((tok, columns), jnp.bfloat16),
        in_specs=[
            pl.BlockSpec(memory_space=pltpu.SMEM), vmem, vmem, vmem, vmem,
            pl.BlockSpec(memory_space=pl.ANY),
        ],
        out_specs=vmem,
        scratch_shapes=[
            pltpu.VMEM((groups, 2, (window + 1) * tok, HD), jnp.bfloat16),
            pltpu.VMEM((groups, wide // HD * tok, HD), jnp.bfloat16),
            pltpu.VMEM((heads, groups, tok, wide), jnp.bfloat16),
            pltpu.VMEM((heads * groups, wide, columns), jnp.bfloat16),
            pltpu.VMEM((tok, columns), jnp.float32),
            dma((heads * groups,)),
            dma((window // 2, groups)),
            dma((window // 2, groups)),
            dma((window + 1, groups)),
            dma((heads // 2, groups)),
            dma((groups,)),
            dma((heads // 2, groups)),
            dma((heads, groups)),
        ],
        compiler_params=pltpu.CompilerParams(
            collective_id=0, has_side_effects=True, vmem_limit_bytes=50 * 2**20
        ),
    )(lengths, inverse, queries, key_proj, value_proj, out_weight)


def solution(mesh):
    placed = (P("ctx", "head"), P("ctx", "head"), P("ctx", "head"), P(), P(None, "head"))
    return jax.shard_map(
        functools.partial(on_device, mesh.shape["ctx"], mesh.shape["head"]),
        mesh=mesh, in_specs=placed, out_specs=P("ctx", "head"), check_vma=False,
    )
```

time: 119 us -> 29.1 us (0.24); the launches traced: 117 us -> 28.9 us
  blocking collectives: 49 us -> 0 us
  waiting for transfers between devices: 32.2 us -> 0 us
  Pallas kernels: 0 us -> 24.7 us
  matrix products: 15.4 us -> 0 us
  between operations: 13.5 us -> 0.01 us
  other arithmetic: 4.3 us -> 0.08 us
  local copies, waits for them, and re-layouts: 2.66 us -> 4.08 us
    all_gather x2 -> x0, blocking collectives: 49 us -> none  [the longest x1 26 us: on_device(): value_part = lax.all_gather(value_proj, 'ctx', axis=0, tiled=True)]
    all_gather x1 -> x0, waiting for transfers between devices: 32.2 us -> none  [on_device(): lax.all_gather(attended, 'head', axis=1, tiled=True)]
    pallas_call x0 -> x1, Pallas kernels: none -> 24.7 us  [on_device(): pl.pallas_call(functools.partial(kernel, n, heads, window), out_shape=jax...]
    dot_general x2 -> x0, matrix products: 11.9 us -> none  [the longest x1 9.26 us: on_device(): jnp.dot(lax.all_gather(attended, 'head', axis=1, tiled=True), out_weight,...]
    cond x1 -> x0, matrix products: 3.43 us -> none  [on_device(): state = lax.cond(needed, update, lambda state: state, initial)]
    unnamed x2 -> x9, local copies, waits for them, and re-layouts: 1.13 us -> 4.08 us
    reduce_sum x2 -> x0, other arithmetic: 1.76 us -> none  [the longest x1 1.02 us: update(): new_sum = jnp.sum(weights, axis=-1)]
  transfers between devices with their start and end apart: 1 -> 0, of which waited for: 1 -> 0; matrix products, arithmetic and copies ran while one was open for 0% -> 0% of each run, Pallas kernels for 0% -> 0%
where the time goes in v1:
time: 29.1 us; the launch traced here: 28.9 us
  Pallas kernels  24.7 us (85%)
  local copies, waits for them, and re-layouts  4.08 us (14%)
    pallas_call x1, Pallas kernels, on_device(): pl.pallas_call(functools.partial(kernel, n, heads, window), out_shape=jax...  24.7 us
    unnamed x9, local copies, waits for them, and re-layouts  4.08 us

profile of v1, /device:TPU:25, one launch (start us, length us, event | category | flops | bytes accessed | tf_op | source)
XLA Modules:
  0.0 28.9 jit_solution(16099610750330468357)
XLA Ops:
  0.0 0.1 maximum_bitcast_fusion.inverse
  0.1 0.0 copy-start
  0.1 1.0 %copy-done = bf16[128,1024]{1,0:T(8,128)(2,1)S(1)} copy-done((bf16[128,1024]{1,0:T(8,128)(2,1)S(1)}, bf16[128,1024]{1,0:T(8,128)(2,1)}, u32[]{:S(2)}) %copy-start) | copy-done | bytes 262168
  1.0 0.0 copy-start.1
  1.0 0.8 %copy-done.1 = bf16[128,256]{1,0:T(8,128)(2,1)S(1)} copy-done((bf16[128,256]{1,0:T(8,128)(2,1)S(1)}, bf16[128,256]{1,0:T(8,128)(2,1)}, u32[]{:S(2)}) %copy-start.1) | copy-done | bytes 65560
  1.9 0.0 copy-start.2
  1.9 0.8 %copy-done.2 = bf16[128,256]{1,0:T(8,128)(2,1)S(1)} copy-done((bf16[128,256]{1,0:T(8,128)(2,1)S(1)}, bf16[128,256]{1,0:T(8,128)(2,1)}, u32[]{:S(2)}) %copy-start.2) | copy-done | bytes 65560
  2.7 0.0 copy-start.3
  2.7 0.7 %copy-done.3 = s32[8]{0:T(128)S(1)} copy-done((s32[8]{0:T(128)S(1)}, s32[8]{0:T(128)}, u32[]{:S(2)}) %copy-start.3) | copy-done | bytes 56
  3.4 24.7 %shard_map.55 = bf16[128,2048]{1,0:T(8,128)(2,1)S(1)} custom-call(s32[8]{0:T(128)S(1)} %copy-done.3, f32[1,128]{1,0:T(1,128)S(1)} %maximum_bitcast_fusion.inverse, bf16[128,1024]{1,0:T(8,128)(2,1)S(1)} %copy-done, bf16[128,256]{1,0:T(8,128)(2,1)S(1)} %copy-done.1, bf16[128,256]{1,0:T(8,128)(2,1)S(1)} %copy-done.2, bf16[4096,2048]{1,0:T(8,128)(2,1)} %w_hbm.1), custom_call_target="tpu_custom_call" | custom-call | tf_op jit(solution)/shard_map/pallas_call | solution.py:253
  28.1 0.8 %copy.7 = bf16[128,2048]{1,0:T(8,128)(2,1)} copy(bf16[128,2048]{1,0:T(8,128)(2,1)S(1)} %shard_map.55) | data formatting | bytes 1048576
  (1 shorter events, 0.0 us)
Async XLA Ops:
  0.1 1.0 %copy-start = (bf16[128,1024]{1,0:T(8,128)(2,1)S(1)}, bf16[128,1024]{1,0:T(8,128)(2,1)}, u32[]{:S(2)}) copy-start(bf16[128,1024]{1,0:T(8,128)(2,1)} %q_in.1) | copy-start | bytes 786436
  1.0 0.8 %copy-start.1 = (bf16[128,256]{1,0:T(8,128)(2,1)S(1)}, bf16[128,256]{1,0:T(8,128)(2,1)}, u32[]{:S(2)}) copy-start(bf16[128,256]{1,0:T(8,128)(2,1)} %k_in.1) | copy-start | bytes 196612
  1.9 0.8 %copy-start.2 = (bf16[128,256]{1,0:T(8,128)(2,1)S(1)}, bf16[128,256]{1,0:T(8,128)(2,1)}, u32[]{:S(2)}) copy-start(bf16[128,256]{1,0:T(8,128)(2,1)} %v_in.1) | copy-start | bytes 196612
  2.7 0.7 %copy-start.3 = (s32[8]{0:T(128)S(1)}, s32[8]{0:T(128)}, u32[]{:S(2)}) copy-start(s32[8]{0:T(128)} %lengths.1) | copy-start | bytes 100

commit v2 on v1

--- a/solution.py
+++ b/solution.py
@@ -13,15 +13,16 @@
 
 
 def kernel(
-    n, heads, window, lengths, inverse, q_in, k_in, v_in, w_hbm, out,
-    kv, q_rot, att, w, acc,
-    w_sem, z_send, y_send, kv_recv, x_send, s_send, r_send, att_recv,
+    n, heads, window, lengths_hbm, inverse_hbm, q_hbm, k_hbm, v_hbm, w_hbm, out,
+    lengths, inverse, q_in, k_in, kv, q_rot, att, w, acc,
+    in_sem, v_sem, w_sem, z_send, y_send, kv_recv, x_send, s_send, r_send, att_recv,
 ):
     tok = q_in.shape[0]
     groups = k_in.shape[1] // HD
     per = q_in.shape[1] // k_in.shape[1]
     wide = per * HD
     steps = window // 2
+    parts = 2 * groups
     chips = heads // 2
     ctx, head = lax.axis_index("ctx"), lax.axis_index("head")
     col, core = lax.rem(ctx, 2), lax.rem(head, 2)
@@ -39,17 +40,31 @@
     greet(ctx, sibling)
     for s in range(1, chips):
         greet(ctx, lax.rem(chip + s, chips) * 2 + core)
-    for k in range(1, steps + 1):
-        up, down = ctx + 2 * k < n, ctx - 2 * k >= 0
-        expected = expected + up.astype(jnp.int32) + down.astype(jnp.int32)
-
-        @pl.when(up)
-        def _():
-            greet(ctx + 2 * k, head)
-
-        @pl.when(down)
-        def _():
-            greet(ctx - 2 * k, head)
+    up, down = ctx + 2 < n, ctx - 2 >= 0
+    expected = expected + up.astype(jnp.int32) + down.astype(jnp.int32)
+
+    @pl.when(up)
+    def _():
+        greet(ctx + 2, head)
+
+    @pl.when(down)
+    def _():
+        greet(ctx - 2, head)
+
+    own = [
+        pltpu.make_async_copy(src, dst, in_sem.at[i])
+        for i, (src, dst) in enumerate(
+            [(lengths_hbm, lengths), (inverse_hbm, inverse), (k_hbm, k_in), (q_hbm, q_in)]
+        )
+    ]
+    values = [
+        pltpu.make_async_copy(
+            v_hbm.at[:, pl.ds(g * HD, HD)], kv.at[g, 1, pl.ds(0, tok), :], v_sem.at[g]
+        )
+        for g in range(groups)
+    ]
+    for copy in own[:3] + values + own[3:]:
+        copy.start()
 
     def weight_copy(h, g):
         piece = h * groups + g
@@ -61,10 +76,8 @@
         order.append(lax.rem(chip + s, chips) * 2 + core)
     for s in range(chips):
         order.append(lax.rem(chip + s, chips) * 2 + 1 - core)
-    for h in order:
-        for g in range(groups):
-            weight_copy(h, g).start()
-
+    own[0].wait()
+    own[1].wait()
     pos = ctx * tok + lax.broadcasted_iota(jnp.int32, (tok, HD), 0)
     starts = jnp.zeros((tok, HD), jnp.int32)
     end = jnp.int32(0)
@@ -81,19 +94,19 @@
         x = x.astype(jnp.float32)
         return (x * cosine + pltpu.roll(x, HD // 2, 1) * sine).astype(jnp.bfloat16)
 
+    own[2].wait()
     for g in range(groups):
-        cols = pl.ds(g * HD, HD)
-        kv[g, 0, pl.ds(0, tok), :] = rotate(k_in[:, cols])
-        kv[g, 1, pl.ds(0, tok), :] = v_in[:, cols]
+        kv[g, 0, pl.ds(0, tok), :] = rotate(k_in[:, pl.ds(g * HD, HD)])
+        values[g].wait()
 
     def slot(g, d):
         return kv.at[g, :, pl.ds(pl.multiple_of(d * tok, tok), tok), :]
 
     def z_copy(k, g):
         return pltpu.make_async_remote_copy(
-            src_ref=slot(g, 0), dst_ref=slot(g, 2 * k),
+            src_ref=slot(g, 2 * k - 2), dst_ref=slot(g, 2 * k),
             send_sem=z_send.at[k - 1, g], recv_sem=kv_recv.at[2 * k, g],
-            device_id=(ctx + 2 * k, head), device_id_type=MESH,
+            device_id=(ctx + 2, head), device_id_type=MESH,
         )
 
     def y_copy(m, g):
@@ -106,15 +119,18 @@
     pl.semaphore_wait(barrier, expected)
 
     for g in range(groups):
-        for k in range(1, steps + 1):
-
-            @pl.when(ctx + 2 * k < n)
-            def _():
-                z_copy(k, g).start()
+
+        @pl.when(up)
+        def _():
+            z_copy(1, g).start()
 
         @pl.when(col == 0)
         def _():
             y_copy(0, g).start()
+
+    for h in order:
+        for g in range(groups):
+            weight_copy(h, g).start()
 
     for d in range(1, window + 1):
 
@@ -123,26 +139,31 @@
             for g in range(groups):
                 kv[g, :, pl.ds(d * tok, tok), :] = jnp.zeros((2, tok, HD), jnp.bfloat16)
 
+    own[3].wait()
     for j in range(groups * per):
         g, r = divmod(j, per)
         q_rot[g, pl.ds(r * tok, tok), :] = rotate(q_in[:, pl.ds(j * HD, HD)])
 
-    def relay(g):
-        for k in range(1, steps + 1):
-
-            @pl.when(ctx - 2 * k >= 0)
-            def _():
-                z_copy(k, g).wait_recv()
-
-            if k <= steps - 1:
-
-                @pl.when((col == 0) & (ctx - 2 * k >= 0))
-                def _():
-                    y_copy(k, g).start()
-
-            @pl.when((col == 1) & (ctx - 2 * k >= 0))
-            def _():
-                y_copy(k - 1, g).start()
+    def relay(k, g):
+        here = ctx - 2 * k >= 0
+
+        @pl.when(here)
+        def _():
+            z_copy(k, g).wait_recv()
+
+        if k < steps:
+
+            @pl.when(here & up)
+            def _():
+                z_copy(k + 1, g).start()
+
+            @pl.when(here & (col == 0))
+            def _():
+                y_copy(k, g).start()
+
+        @pl.when(here & (col == 1))
+        def _():
+            y_copy(k - 1, g).start()
 
     keys = (window + 1) * tok
     spot = lax.broadcasted_iota(jnp.int32, (tok, keys), 1)
@@ -168,7 +189,10 @@
             mixed = jnp.dot(
                 expo.astype(jnp.bfloat16), kv[g, 1], preferred_element_type=jnp.float32
             )
-            att[head, g, :, pl.ds(r * HD, HD)] = (mixed / total).astype(jnp.bfloat16)
+            p, place = divmod(r, per // 2)
+            att[head, 2 * g + p, :, pl.ds(place * HD, HD)] = (mixed / total).astype(jnp.bfloat16)
+            if place == per // 2 - 1:
+                share(2 * g + p)
 
     def x_copy(s, g):
         return pltpu.make_async_remote_copy(
@@ -192,38 +216,44 @@
             x_copy(s, g).start()
         core_copy(head, g, s_send.at[g]).start()
 
-    def project(h, g, first=False):
-        weight_copy(h, g).wait()
-        part = jnp.dot(att[h, g], w[h * groups + g], preferred_element_type=jnp.float32)
+    def project(h, b, first=False):
+        if b % 2 == 0:
+            weight_copy(h, b // 2).wait()
+        rows = w[h * groups + b // 2, pl.ds(b % 2 * (wide // 2), wide // 2), :]
+        part = jnp.dot(att[h, b], rows, preferred_element_type=jnp.float32)
         acc[...] = part if first else acc[...] + part
 
-    relay(0)
+    for k in range(1, steps + 1):
+        for g in range(groups):
+            relay(k, g)
     for g in range(groups):
-        if g + 1 < groups:
-            relay(g + 1)
         attend(g)
-        share(g)
-    for g in range(groups):
-        project(head, g, first=g == 0)
-    for g in range(groups):
-        arrived(sibling, g)
-        project(sibling, g)
-    for g in range(groups):
-        for s in range(1, chips):
-            h = order[s]
-            arrived(h, g)
-            core_copy(h, g, r_send.at[s - 1, g]).start()
-            project(h, g)
+    def forward(b):
+        for s in range(1, chips):
+            arrived(order[s], b)
+            core_copy(order[s], b, r_send.at[s - 1, b]).start()
+
+    for b in range(parts):
+        project(head, b, first=b == 0)
+    for b in range(parts):
+        arrived(sibling, b)
+        project(sibling, b)
+    forward(0)
+    for b in range(parts):
+        for s in range(1, chips):
+            project(order[s], b)
+        if b + 1 < parts:
+            forward(b + 1)
         for s in range(1, chips):
             h = order[chips + s]
-            arrived(h, g)
-            project(h, g)
+            arrived(h, b)
+            project(h, b)
     out[...] = acc[...].astype(out.dtype)
 
     for g in range(groups):
         for k in range(1, steps + 1):
 
-            @pl.when(ctx + 2 * k < n)
+            @pl.when(up & (ctx - 2 * k + 2 >= 0))
             def _():
                 z_copy(k, g).wait_send()
 
@@ -233,10 +263,11 @@
             def _():
                 y_copy(m, g).wait_send()
 
-        for s in range(1, chips):
-            x_copy(s, g).wait_send()
-            core_copy(order[s], g, r_send.at[s - 1, g]).wait_send()
-        core_copy(head, g, s_send.at[g]).wait_send()
+    for b in range(parts):
+        for s in range(1, chips):
+            x_copy(s, b).wait_send()
+            core_copy(order[s], b, r_send.at[s - 1, b]).wait_send()
+        core_copy(head, b, s_send.at[b]).wait_send()
 
 
 def on_device(n, heads, queries, key_proj, value_proj, lengths, out_weight):
@@ -253,28 +284,31 @@
     return pl.pallas_call(
         functools.partial(kernel, n, heads, window),
         out_shape=jax.ShapeDtypeStruct((tok, columns), jnp.bfloat16),
-        in_specs=[
-            pl.BlockSpec(memory_space=pltpu.SMEM), vmem, vmem, vmem, vmem,
-            pl.BlockSpec(memory_space=pl.ANY),
-        ],
+        in_specs=[pl.BlockSpec(memory_space=pltpu.HBM)] * 6,
         out_specs=vmem,
         scratch_shapes=[
+            pltpu.SMEM(lengths.shape, jnp.int32),
+            pltpu.VMEM(inverse.shape, jnp.float32),
+            pltpu.VMEM(queries.shape, jnp.bfloat16),
+            pltpu.VMEM(key_proj.shape, jnp.bfloat16),
             pltpu.VMEM((groups, 2, (window + 1) * tok, HD), jnp.bfloat16),
             pltpu.VMEM((groups, wide // HD * tok, HD), jnp.bfloat16),
-            pltpu.VMEM((heads, groups, tok, wide), jnp.bfloat16),
+            pltpu.VMEM((heads, 2 * groups, tok, wide // 2), jnp.bfloat16),
             pltpu.VMEM((heads * groups, wide, columns), jnp.bfloat16),
             pltpu.VMEM((tok, columns), jnp.float32),
+            dma((4,)),
+            dma((groups,)),
             dma((heads * groups,)),
             dma((window // 2, groups)),
             dma((window // 2, groups)),
             dma((window + 1, groups)),
-            dma((heads // 2, groups)),
-            dma((groups,)),
-            dma((heads // 2, groups)),
-            dma((heads, groups)),
+            dma((heads // 2, 2 * groups)),
+            dma((2 * groups,)),
+            dma((heads // 2, 2 * groups)),
+            dma((heads, 2 * groups)),
         ],
         compiler_params=pltpu.CompilerParams(
-            collective_id=0, has_side_effects=True, vmem_limit_bytes=50 * 2**20
+            collective_id=0, has_side_effects=True, vmem_limit_bytes=63 * 2**20
         ),
     )(lengths, inverse, queries, key_proj, value_proj, out_weight)
 

time: 29.1 us -> 23.9 us (0.82)
  Pallas kernels: 24.7 us -> 21.3 us
  local copies, waits for them, and re-layouts: 4.08 us -> 1.88 us
  other arithmetic: 0.08 us -> 0.6 us
    pallas_call x1, Pallas kernels: 24.7 us -> 21.3 us  [on_device(): pl.pallas_call(functools.partial(kernel, n, heads, window), out_shape=jax...]
    unnamed x9 -> x1, local copies, waits for them, and re-layouts: 4.08 us -> 1.88 us
    broadcast_in_dim x1, other arithmetic: 0.08 us -> 0.59 us  [on_device(): inverse = jnp.concatenate([inverse, inverse])[None, :]]
where the time goes in v2:
time: 23.9 us; the launch traced here: 23.8 us
  Pallas kernels  21.3 us (89%)
  local copies, waits for them, and re-layouts  1.88 us (8%)
  other arithmetic  0.6 us (3%)
    pallas_call x1, Pallas kernels, on_device(): pl.pallas_call(functools.partial(kernel, n, heads, window), out_shape=jax...  21.3 us
    unnamed x1, local copies, waits for them, and re-layouts  1.88 us
    broadcast_in_dim x1, other arithmetic, on_device(): inverse = jnp.concatenate([inverse, inverse])[None, :]  0.59 us

profile of v2, /device:TPU:25, one launch (start us, length us, event | category | flops | bytes accessed | tf_op | source)
XLA Modules:
  0.0 23.8 jit_solution(6488150249551887202)
XLA Ops:
  0.0 0.6 %maximum_bitcast_fusion.inverse_hbm = f32[1,128]{1,0:T(1,128)} fusion(f32[64]{0:T(128)S(1)} %multiply_power_fusion), kind=kLoop, calls=%fused_computation | loop fusion | flops 128 | bytes 768 | tf_op jit(solution)/shard_map/broadcast_in_dim | solution.py:281
  0.6 21.3 %shard_map.55 = bf16[128,2048]{1,0:T(8,128)(2,1)} custom-call(s32[8]{0:T(128)} %lengths_hbm.1, f32[1,128]{1,0:T(1,128)} %maximum_bitcast_fusion.inverse_hbm, bf16[128,1024]{1,0:T(8,128)(2,1)} %q_hbm.1, bf16[128,256]{1,0:T(8,128)(2,1)} %k_hbm.1, bf16[128,256]{1,0:T(8,128)(2,1)} %v_hbm.1, bf16[4096,2048]{1,0:T(8,128)(2,1)} %w_hbm.1), custom_call_target="tpu_custom_call" | custom-call | tf_op jit(solution)/shard_map/pallas_call | solution.py:284
  21.9 1.9 %copy.7 = bf16[128,2048]{1,0:T(8,128)(2,1)} copy(bf16[128,2048]{1,0:T(8,128)(2,1)} %shard_map.55) | data formatting | bytes 1048576
  (1 shorter events, 0.0 us)
